TPU v7x, 512 devices: a whole 4x4x16 slice. The times are simulated.
512 devices in a mesh: blk: 128 (over y, z_lo, x), feat: 4 (over z_hi, core).
Axes of the slice: x: 4, y: 4, z: 16 (z_hi: 2, z_lo: 8; z = z_hi * 8 + z_lo), core: 2. Of those that a mesh axis runs over, the one named last changes fastest.
Arguments:
- features: bfloat16 [131072, 512], P('blk', 'feat')
- hop_noise: bfloat16 [2, 131072, 512], P(None, 'blk', 'feat'), may hold values from -4 to 4
- encoder_weight: bfloat16 [2, 512, 512], replicated, may hold values from -0.03125 to 0.03125
- block_target: int32 [128, 40], P('blk'), may hold values from 0 to 7
- block_source: int32 [128, 40], P('blk'), may hold values from 0 to 39
- block_count: int32 [128], P('blk'), may hold values from 10 to 40
- tile_mask: int32 [128, 40, 128, 128], P('blk'), may hold values 0 or 1
Outputs:
- encoded_one: bfloat16 [131072, 512], P('blk', 'feat')
- encoded_two: bfloat16 [131072, 512], P('blk', 'feat')
Inputs may be any that keep to these rules, and one draw needn't show every extreme that they name: Entries k < block_count of a partition's list are live, the others are ignored. `block_source`: window index: source partition offset index // 8 - 2, row block index % 8.
All inputs are finite; a program needn't handle non-finite values. No bound on the sum of `tile_mask` on one device may be relied on, other than what follows from the above.
Results may differ from a plain program's by a relative error of at most 0.015.
Values may be sent and summed in bfloat16 or wider, within the bound.
A program may use at most 64 MiB of HBM per device.

v0:
```python
import jax
import jax.numpy as jnp
from jax import lax
from jax.sharding import PartitionSpec as P

TILE = 128
TILES = 8
HALF = 2
K = 40
HOPS = 2


def passed_along(x, axis, by):
    size = lax.axis_size(axis)
    return lax.ppermute(x, axis, [(i, (i + by) % size) for i in range(size)])


def band_window(clipped):
    above = []
    moving = clipped
    for offset in range(HALF):
        moving = passed_along(moving, "blk", -1)
        above.append(moving)
    below = []
    moving = clipped
    for offset in range(HALF):
        moving = passed_along(moving, "blk", 1)
        below.append(moving)
    return below[::-1] + [clipped] + above


def encode_rows(noisy, weight, columns):
    my_first = lax.axis_index("feat") * columns
    my_columns = lax.dynamic_slice_in_dim(weight, my_first, columns, 1)
    summed = jnp.dot(
        lax.all_gather(noisy, "feat", axis=1, tiled=True),
        my_columns,
        preferred_element_type=jnp.float32,
    )
    return summed.astype(jnp.bfloat16)


def per_device(
    features, hop_noise, encoder_weight, block_target, block_source, block_count, tile_mask
):
    row_count = features.shape[0]
    columns = features.shape[1]
    mask_values = tile_mask[0].astype(jnp.bfloat16)
    targets = block_target[0]
    sources = block_source[0]
    active = jnp.arange(K) < block_count[0]
    routing = ((targets[:, None] == jnp.arange(TILES)[None, :]) & active[:, None]).astype(
        jnp.float32
    )
    current = features
    results = []
    for hop_index in range(HOPS):
        widened = current.astype(jnp.float32)
        squares = lax.psum(jnp.sum(widened * widened, axis=1), "feat")
        clipped = (widened / jnp.maximum(1.0, jnp.sqrt(squares))[:, None]).astype(jnp.bfloat16)
        window_tiles = jnp.concatenate(band_window(clipped), axis=0).reshape(-1, TILE, columns)
        picked = window_tiles[sources]
        products = jnp.einsum(
            "kij,kjf->kif", mask_values, picked, preferred_element_type=jnp.float32
        )
        aggregate = jnp.einsum("kt,kif->tif", routing, products).reshape(row_count, columns)
        noisy = (aggregate + hop_noise[hop_index].astype(jnp.float32)).astype(jnp.bfloat16)
        encoded = encode_rows(noisy, encoder_weight[hop_index], columns)
        results.append(encoded)
        current = encoded
    return (results[0], results[1])


def solution(mesh):
    in_specs = (
        P("blk", "feat"),
        P(None, "blk", "feat"),
        P(),
        P("blk", None),
        P("blk", None),
        P("blk"),
        P("blk", None, None, None),
    )
    out_specs = (P("blk", "feat"), P("blk", "feat"))
    return jax.shard_map(
        per_device, mesh=mesh, in_specs=in_specs, out_specs=out_specs, check_vma=False
    )
```

profile of v0, /device:TPU:1, one launch (start us, length us, event | category | flops | bytes accessed | tf_op | source)
XLA Modules:
  0.0 276.7 jit_solution(6634274752078948736)
XLA Ops:
  7.2 1.2 fusion.10
  8.4 20.6 %psum.14 = f32[1024]{0:T(1024)S(1)} all-reduce(f32[1024]{0:T(1024)S(1)} %fusion.10), channel_id=1, replica_groups=mesh['blk'=128,'feat'=4] {'feat'}, use_global_device_ids=true, to_apply=%region_1.0 | all-reduce | flops 1024 | bytes 8192 | tf_op jit(solution)/shard_map/psum | solution.py:59
  29.0 1.2 fusion.11
  30.2 1.9 collective-permute-start
  32.1 14.2 %collective-permute-start.2 = (bf16[1024,128]{1,0:T(8,128)(2,1)S(1)}, bf16[1024,128]{1,0:T(8,128)(2,1)S(1)}, u32[]{:S(2)}, u32[]{:S(2)}) collective-permute-start(bf16[1024,128]{1,0:T(8,128)(2,1)S(1)} %fusion.11), channel_id=1, source_target_pairs={{0,508},{4,0},{8,4},{12,8},{16,12},{20,16},{24,20},{28,24},{32,28}... | collective-permute-start | bytes 786440 | tf_op jit(solution)/shard_map/ppermute | solution.py:15
  46.3 1.8 collective-permute-done
  48.2 1.9 collective-permute-start.1
  51.4 14.2 %collective-permute-start.3 = (bf16[1024,128]{1,0:T(8,128)(2,1)S(1)}, bf16[1024,128]{1,0:T(8,128)(2,1)S(1)}, u32[]{:S(2)}, u32[]{:S(2)}) collective-permute-start(bf16[1024,128]{1,0:T(8,128)(2,1)S(1)} %collective-permute-done.2), channel_id=1, source_target_pairs={{0,508},{4,0},{8,4},{12,8},{16,12},{20,16},{24,20},{28,24},{32,28}... | collective-permute-start | bytes 786440 | tf_op jit(solution)/shard_map/ppermute | solution.py:15
  66.5 2.4 collective-permute-done.3
  69.0 1.0 copy-done.2
  70.0 3.3 %gather_fusion = bf16[40,128,128]{2,1,0:T(8,128)(2,1)} fusion(bf16[40,128,128]{2,1,0:T(8,128)(2,1)} %bitcast.46, s32[1024]{0:T(1024)S(1)} %pad_clamp_fusion), kind=kCustom, calls=%fused_computation | custom fusion | bytes 2621600 | tf_op jit(solution)/shard_map/gather | solution.py:62
  73.4 3.4 %fusion.6 = bf16[40,128,128]{2,1,0:T(8,128)(2,1)} fusion(bf16[40,128,128]{2,1,0:T(8,128)(2,1)} %gather_fusion, s32[1,40,128,128]{3,2,1,0:T(8,128)S(1)} %copy-done), kind=kOutput, calls=%fused_computation.8 | convolution fusion | flops 168427520 | bytes 5242880 | tf_op jit(solution)/shard_map/kij,kjf->kif/dot_general | solution.py:63
  76.8 2.7 copy.11
  79.5 1.7 fusion.2
  81.4 0.8 fusion.15
  82.2 2.1 fusion.31
  84.3 61.0 %all-gather.3.cloned.1.call-done = bf16[1024,512]{1,0:T(8,128)(2,1)} async-done(((bf16[1024,128]{1,0:T(8,128)(2,1)}), bf16[1024,512]{1,0:T(8,128)(2,1)}) %all-gather.3.cloned.1.call-update) | async-done | bytes 1048592 | tf_op jit(solution)/shard_map/all_gather | solution.py:36
  145.3 1.7 fusion.12
  147.1 14.0 %psum.15 = f32[1024]{0:T(1024)S(1)} all-reduce(f32[1024]{0:T(1024)S(1)} %get-tuple-element.4), channel_id=1, replica_groups=mesh['blk'=128,'feat'=4] {'feat'}, use_global_device_ids=true, to_apply=%region_3.0 | all-reduce | flops 1024 | bytes 8192 | tf_op jit(solution)/shard_map/psum | solution.py:59
  161.3 3.1 %collective-permute-start.4 = (bf16[1024,128]{1,0:T(8,128)(2,1)S(1)}, bf16[1024,128]{1,0:T(8,128)(2,1)S(1)}, u32[]{:S(2)}, u32[]{:S(2)}) collective-permute-start(bf16[1024,128]{1,0:T(8,128)(2,1)S(1)} %fusion.13), channel_id=1, source_target_pairs={{0,4},{4,8},{8,12},{12,16},{16,20},{20,24},{24,28},{28,32},{32,36}... | collective-permute-start | bytes 786440 | tf_op jit(solution)/shard_map/ppermute | solution.py:15
  164.4 13.0 %collective-permute-start.6 = (bf16[1024,128]{1,0:T(8,128)(2,1)S(1)}, bf16[1024,128]{1,0:T(8,128)(2,1)S(1)}, u32[]{:S(2)}, u32[]{:S(2)}) collective-permute-start(bf16[1024,128]{1,0:T(8,128)(2,1)S(1)} %fusion.13), channel_id=1, source_target_pairs={{0,508},{4,0},{8,4},{12,8},{16,12},{20,16},{24,20},{28,24},{32,28}... | collective-permute-start | bytes 786440 | tf_op jit(solution)/shard_map/ppermute | solution.py:15
  177.4 3.5 %collective-permute-done.4 = bf16[1024,128]{1,0:T(8,128)(2,1)S(1)} collective-permute-done((bf16[1024,128]{1,0:T(8,128)(2,1)S(1)}, bf16[1024,128]{1,0:T(8,128)(2,1)S(1)}, u32[]{:S(2)}, u32[]{:S(2)}) %collective-permute-start.4) | collective-permute-done | bytes 262176 | tf_op jit(solution)/shard_map/ppermute | solution.py:15
  180.9 1.9 collective-permute-start.5
  182.9 14.2 %collective-permute-start.7 = (bf16[1024,128]{1,0:T(8,128)(2,1)S(1)}, bf16[1024,128]{1,0:T(8,128)(2,1)S(1)}, u32[]{:S(2)}, u32[]{:S(2)}) collective-permute-start(bf16[1024,128]{1,0:T(8,128)(2,1)S(1)} %collective-permute-done.6), channel_id=1, source_target_pairs={{0,508},{4,0},{8,4},{12,8},{16,12},{20,16},{24,20},{28,24},{32,28}... | collective-permute-start | bytes 786440 | tf_op jit(solution)/shard_map/ppermute | solution.py:15
  197.1 2.6 collective-permute-done.5
  201.1 0.9 constant_dynamic-update-slice_fusion.7
  203.4 3.2 %gather_fusion.1 = bf16[40,128,128]{2,1,0:T(8,128)(2,1)} fusion(bf16[40,128,128]{2,1,0:T(8,128)(2,1)} %bitcast.11, s32[1024]{0:T(1024)S(1)} %pad_clamp_fusion), kind=kCustom, calls=%fused_computation.1 | custom fusion | bytes 2621600 | tf_op jit(solution)/shard_map/gather | solution.py:62
  206.6 3.4 %fusion.4 = bf16[40,128,128]{2,1,0:T(8,128)(2,1)} fusion(bf16[40,128,128]{2,1,0:T(8,128)(2,1)} %gather_fusion.1, s32[1,40,128,128]{3,2,1,0:T(8,128)S(1)} %copy-done), kind=kOutput, calls=%fused_computation.6 | convolution fusion | flops 168427520 | bytes 5242880 | tf_op jit(solution)/shard_map/kij,kjf->kif/dot_general | solution.py:63
  210.1 2.1 copy.12
  213.3 0.8 fusion.14
  214.1 53.4 %all-gather.5.cloned.1.call-done = bf16[1024,512]{1,0:T(8,128)(2,1)} async-done(((bf16[1024,128]{1,0:T(8,128)(2,1)}), bf16[1024,512]{1,0:T(8,128)(2,1)}) %all-gather.5.cloned.1.call-update) | async-done | bytes 1048592 | tf_op jit(solution)/shard_map/all_gather | solution.py:36
  267.4 2.4 convolution_convert_fusion
  (39 shorter events, 5.9 us)
Async XLA Ops:
  7.2 59.0 %copy-start.1 = (bf16[1024,128]{1,0:T(8,128)(2,1)S(1)}, bf16[1024,128]{1,0:T(8,128)(2,1)}, u32[]{:S(2)}) copy-start(bf16[1024,128]{1,0:T(8,128)(2,1)} %param.7) | copy-start | bytes 786436
  7.2 138.1 %all-gather.3.cloned.1.call-start = ((), (), s32[]{:S(2)}) async-start(), calls=%async_computation | async-start | bytes 1310720 | tf_op jit(solution)/shard_map/all_gather | solution.py:36
  30.2 17.9 %collective-permute-start = (bf16[1024,128]{1,0:T(8,128)(2,1)S(1)}, bf16[1024,128]{1,0:T(8,128)(2,1)S(1)}, u32[]{:S(2)}, u32[]{:S(2)}) collective-permute-start(bf16[1024,128]{1,0:T(8,128)(2,1)S(1)} %fusion.11), channel_id=1, source_target_pairs={{0,4},{4,8},{8,12},{12,16},{16,20},{20,24},{24,28},{28,32},{32,36}... | collective-permute-start | bytes 786440 | tf_op jit(solution)/shard_map/ppermute | solution.py:15
  32.1 19.3 %collective-permute-start.2 = (bf16[1024,128]{1,0:T(8,128)(2,1)S(1)}, bf16[1024,128]{1,0:T(8,128)(2,1)S(1)}, u32[]{:S(2)}, u32[]{:S(2)}) collective-permute-start(bf16[1024,128]{1,0:T(8,128)(2,1)S(1)} %fusion.11), channel_id=1, source_target_pairs={{0,508},{4,0},{8,4},{12,8},{16,12},{20,16},{24,20},{28,24},{32,28}... | collective-permute-start | bytes 786440 | tf_op jit(solution)/shard_map/ppermute | solution.py:15
  48.2 17.9 %collective-permute-start.1 = (bf16[1024,128]{1,0:T(8,128)(2,1)S(1)}, bf16[1024,128]{1,0:T(8,128)(2,1)S(1)}, u32[]{:S(2)}, u32[]{:S(2)}) collective-permute-start(bf16[1024,128]{1,0:T(8,128)(2,1)S(1)} %collective-permute-done), channel_id=1, source_target_pairs={{0,4},{4,8},{8,12},{12,16},{16,20},{20,24},{24,28},{28,32},{32,36}... | collective-permute-start | bytes 786440 | tf_op jit(solution)/shard_map/ppermute | solution.py:15
  51.4 17.5 %collective-permute-start.3 = (bf16[1024,128]{1,0:T(8,128)(2,1)S(1)}, bf16[1024,128]{1,0:T(8,128)(2,1)S(1)}, u32[]{:S(2)}, u32[]{:S(2)}) collective-permute-start(bf16[1024,128]{1,0:T(8,128)(2,1)S(1)} %collective-permute-done.2), channel_id=1, source_target_pairs={{0,508},{4,0},{8,4},{12,8},{16,12},{20,16},{24,20},{28,24},{32,28}... | collective-permute-start | bytes 786440 | tf_op jit(solution)/shard_map/ppermute | solution.py:15
  68.9 1.1 copy-start.2
  70.0 3.4 %copy-start = (s32[1,40,128,128]{3,2,1,0:T(8,128)S(1)}, s32[1,40,128,128]{3,2,1,0:T(8,128)}, u32[]{:S(2)}) copy-start(s32[1,40,128,128]{3,2,1,0:T(8,128)} %param.13) | copy-start | bytes 7864324
  76.8 2.8 copy-start.6
  79.5 1.8 copy-start.4
  82.2 185.3 %all-gather.5.cloned.1.call-start = ((), (), s32[]{:S(2)}) async-start(), calls=%async_computation.1 | async-start | bytes 1310720 | tf_op jit(solution)/shard_map/all_gather | solution.py:36
  147.0 55.7 %copy-start.3 = (bf16[1024,128]{1,0:T(8,128)(2,1)}, bf16[1024,128]{1,0:T(8,128)(2,1)S(1)}, u32[]{:S(2)}) copy-start(bf16[1024,128]{1,0:T(8,128)(2,1)S(1)} %get-tuple-element.5) | copy-start | bytes 786436
  161.3 19.6 %collective-permute-start.4 = (bf16[1024,128]{1,0:T(8,128)(2,1)S(1)}, bf16[1024,128]{1,0:T(8,128)(2,1)S(1)}, u32[]{:S(2)}, u32[]{:S(2)}) collective-permute-start(bf16[1024,128]{1,0:T(8,128)(2,1)S(1)} %fusion.13), channel_id=1, source_target_pairs={{0,4},{4,8},{8,12},{12,16},{16,20},{20,24},{24,28},{28,32},{32,36}... | collective-permute-start | bytes 786440 | tf_op jit(solution)/shard_map/ppermute | solution.py:15
  164.4 18.4 %collective-permute-start.6 = (bf16[1024,128]{1,0:T(8,128)(2,1)S(1)}, bf16[1024,128]{1,0:T(8,128)(2,1)S(1)}, u32[]{:S(2)}, u32[]{:S(2)}) collective-permute-start(bf16[1024,128]{1,0:T(8,128)(2,1)S(1)} %fusion.13), channel_id=1, source_target_pairs={{0,508},{4,0},{8,4},{12,8},{16,12},{20,16},{24,20},{28,24},{32,28}... | collective-permute-start | bytes 786440 | tf_op jit(solution)/shard_map/ppermute | solution.py:15
  180.9 18.7 %collective-permute-start.5 = (bf16[1024,128]{1,0:T(8,128)(2,1)S(1)}, bf16[1024,128]{1,0:T(8,128)(2,1)S(1)}, u32[]{:S(2)}, u32[]{:S(2)}) collective-permute-start(bf16[1024,128]{1,0:T(8,128)(2,1)S(1)} %collective-permute-done.4), channel_id=1, source_target_pairs={{0,4},{4,8},{8,12},{12,16},{16,20},{20,24},{24,28},{28,32},{32,36}... | collective-permute-start | bytes 786440 | tf_op jit(solution)/shard_map/ppermute | solution.py:15
  182.9 19.9 %collective-permute-start.7 = (bf16[1024,128]{1,0:T(8,128)(2,1)S(1)}, bf16[1024,128]{1,0:T(8,128)(2,1)S(1)}, u32[]{:S(2)}, u32[]{:S(2)}) collective-permute-start(bf16[1024,128]{1,0:T(8,128)(2,1)S(1)} %collective-permute-done.6), channel_id=1, source_target_pairs={{0,508},{4,0},{8,4},{12,8},{16,12},{20,16},{24,20},{28,24},{32,28}... | collective-permute-start | bytes 786440 | tf_op jit(solution)/shard_map/ppermute | solution.py:15
  212.2 1.0 copy-start.5
Sparse Core Ops, SparseCore 0:
  82.3 62.9 all-gather.2
  214.2 53.2 all-gather.4
where the time goes:
time: 277 us
  waiting for transfers between devices  125 us (45%)
  starting transfers between devices  64.5 us (23%)
  blocking collectives  34.6 us (12%)
  local copies, waits for them, and re-layouts  18.3 us (7%)
  between operations  14.9 us (5%)
  matrix products  13 us (5%)
  other arithmetic  5.97 us (2%)
    all_gather x2, waiting for transfers between devices, encode_rows(): lax.all_gather(noisy, 'feat', axis=1, tiled=True)  114 us
    ppermute x8, starting transfers between devices, passed_along(): return lax.ppermute(x, axis, [(i, (i + by) % size) for i in range(size)])  64.4 us
    psum x2, blocking collectives, per_device(): squares = lax.psum(jnp.sum(widened * widened, axis=1), 'feat')  34.6 us
    ppermute x8, waiting for transfers between devices, passed_along(): return lax.ppermute(x, axis, [(i, (i + by) % size) for i in range(size)])  10.9 us
    dot_general x2, matrix products, per_device(): jnp.einsum('kij,kjf->kif', mask_values, picked, preferred_element_type=jn...  6.87 us
    gather x2, local copies, waits for them, and re-layouts, per_device(): picked = window_tiles[sources]  6.54 us
  transfers between devices with their start and end apart: 10, of which 7 were waited for; matrix products, arithmetic and copies ran while one was open for 2% of the time, Pallas kernels for 0%

commit v1 on v0

--- a/solution.py
+++ b/solution.py
@@ -56,7 +56,7 @@
     results = []
     for hop_index in range(HOPS):
         widened = current.astype(jnp.float32)
-        squares = lax.psum(jnp.sum(widened * widened, axis=1), "feat")
+        squares = jnp.sum(lax.all_gather(jnp.sum(widened * widened, axis=1), "feat"), axis=0)
         clipped = (widened / jnp.maximum(1.0, jnp.sqrt(squares))[:, None]).astype(jnp.bfloat16)
         window_tiles = jnp.concatenate(band_window(clipped), axis=0).reshape(-1, TILE, columns)
         picked = window_tiles[sources]

time: 277 us -> 273 us (0.986)
  waiting for transfers between devices: 125 us -> 120 us
    psum x2 -> x0, blocking collectives: 34.6 us -> none  [per_device(): squares = lax.psum(jnp.sum(widened * widened, axis=1), 'feat')]
    all_gather x0 -> x2, blocking collectives: none -> 34.5 us  [per_device(): lax.all_gather(jnp.sum(widened * widened, axis=1), 'feat')]
    all_gather x2, waiting for transfers between devices: 114 us -> 105 us  [encode_rows(): lax.all_gather(noisy, 'feat', axis=1, tiled=True)]
    ppermute x8, waiting for transfers between devices: 10.9 us -> 15.9 us  [passed_along(): return lax.ppermute(x, axis, [(i, (i + by) % size) for i in range(size)])]
where the time goes in v1:
time: 273 us; the launch traced here: 272 us
  waiting for transfers between devices  120 us (44%)
  starting transfers between devices  64.5 us (24%)
  blocking collectives  34.5 us (13%)
  local copies, waits for them, and re-layouts  18.4 us (7%)
  between operations  14.9 us (5%)
  matrix products  13 us (5%)
  other arithmetic  5.99 us (2%)
    all_gather x2, waiting for transfers between devices, encode_rows(): lax.all_gather(noisy, 'feat', axis=1, tiled=True)  105 us
    ppermute x8, starting transfers between devices, passed_along(): return lax.ppermute(x, axis, [(i, (i + by) % size) for i in range(size)])  64.4 us
    all_gather x2, blocking collectives, per_device(): lax.all_gather(jnp.sum(widened * widened, axis=1), 'feat')  34.5 us
    ppermute x8, waiting for transfers between devices, passed_along(): return lax.ppermute(x, axis, [(i, (i + by) % size) for i in range(size)])  15.9 us
    dot_general x2, matrix products, per_device(): jnp.einsum('kij,kjf->kif', mask_values, picked, preferred_element_type=jn...  6.87 us
    gather x2, local copies, waits for them, and re-layouts, per_device(): picked = window_tiles[sources]  6.54 us
  transfers between devices with their start and end apart: 10, of which 7 were waited for; matrix products, arithmetic and copies ran while one was open for 2% of the time, Pallas kernels for 0%

profile of v1, /device:TPU:1, one launch (start us, length us, event | category | flops | bytes accessed | tf_op | source)
XLA Modules:
  0.0 271.8 jit_solution(5540008915844949775)
XLA Ops:
  7.2 1.2 fusion.4
  8.4 20.6 %all-gather = f32[4096]{0:T(1024)S(1)} all-gather(f32[1024]{0:T(1024)S(1)} %fusion.4), channel_id=2, replica_groups=mesh['blk'=128,'feat'=4] {'feat'}, dimensions={0}, use_global_device_ids=true | all-gather | bytes 20480 | tf_op jit(solution)/shard_map/all_gather | solution.py:59
  29.0 1.2 fusion.5
  30.2 1.9 collective-permute-start
  32.1 14.2 %collective-permute-start.2 = (bf16[1024,128]{1,0:T(8,128)(2,1)S(1)}, bf16[1024,128]{1,0:T(8,128)(2,1)S(1)}, u32[]{:S(2)}, u32[]{:S(2)}) collective-permute-start(bf16[1024,128]{1,0:T(8,128)(2,1)S(1)} %fusion.5), channel_id=1, source_target_pairs={{0,508},{4,0},{8,4},{12,8},{16,12},{20,16},{24,20},{28,24},{32,28}... | collective-permute-start | bytes 786440 | tf_op jit(solution)/shard_map/ppermute | solution.py:15
  46.3 4.3 %collective-permute-done = bf16[1024,128]{1,0:T(8,128)(2,1)S(1)} collective-permute-done((bf16[1024,128]{1,0:T(8,128)(2,1)S(1)}, bf16[1024,128]{1,0:T(8,128)(2,1)S(1)}, u32[]{:S(2)}, u32[]{:S(2)}) %collective-permute-start) | collective-permute-done | bytes 262176 | tf_op jit(solution)/shard_map/ppermute | solution.py:15
  50.6 1.9 collective-permute-start.1
  53.9 14.2 %collective-permute-start.3 = (bf16[1024,128]{1,0:T(8,128)(2,1)S(1)}, bf16[1024,128]{1,0:T(8,128)(2,1)S(1)}, u32[]{:S(2)}, u32[]{:S(2)}) collective-permute-start(bf16[1024,128]{1,0:T(8,128)(2,1)S(1)} %collective-permute-done.2), channel_id=1, source_target_pairs={{0,508},{4,0},{8,4},{12,8},{16,12},{20,16},{24,20},{28,24},{32,28}... | collective-permute-start | bytes 786440 | tf_op jit(solution)/shard_map/ppermute | solution.py:15
  68.1 2.0 collective-permute-done.1
  70.5 1.9 collective-permute-done.3
  72.4 1.0 copy-done.2
  73.5 3.3 %gather_fusion = bf16[40,128,128]{2,1,0:T(8,128)(2,1)} fusion(bf16[40,128,128]{2,1,0:T(8,128)(2,1)} %bitcast.46, s32[1024]{0:T(1024)S(1)} %pad_clamp_fusion), kind=kCustom, calls=%fused_computation | custom fusion | bytes 2621600 | tf_op jit(solution)/shard_map/gather | solution.py:62
  76.8 3.4 %convolution_bitcast_fusion.1 = bf16[40,128,128]{1,2,0:T(8,128)(2,1)} fusion(bf16[40,128,128]{2,1,0:T(8,128)(2,1)} %gather_fusion, s32[1,40,128,128]{3,2,1,0:T(8,128)S(1)} %copy-done), kind=kOutput, calls=%fused_computation.3 | convolution fusion | flops 168427520 | bytes 5242880 | tf_op jit(solution)/shard_map/kij,kjf->kif/dot_general | solution.py:63
  80.3 2.7 %copy.22 = bf16[40,128,128]{2,0,1:T(8,128)(2,1)} copy(bf16[40,128,128]{1,2,0:T(8,128)(2,1)} %convolution_bitcast_fusion.1) | data formatting | bytes 2621440 | tf_op jit(solution)/shard_map/kij,kjf->kif/dot_general | solution.py:63
  83.0 1.7 fusion.18
  85.7 2.1 fusion.27
  87.8 52.5 %all-gather.5.cloned.1.call-done = bf16[1024,512]{1,0:T(8,128)(2,1)} async-done(((bf16[1024,128]{1,0:T(8,128)(2,1)}), bf16[1024,512]{1,0:T(8,128)(2,1)}) %all-gather.5.cloned.1.call-update) | async-done | bytes 1048592 | tf_op jit(solution)/shard_map/all_gather | solution.py:36
  140.2 1.7 fusion.6
  142.0 14.0 %all-gather.1 = f32[4096]{0:T(1024)S(1)} all-gather(f32[1024]{0:T(1024)S(1)} %get-tuple-element.4), channel_id=3, replica_groups=mesh['blk'=128,'feat'=4] {'feat'}, dimensions={0}, use_global_device_ids=true | all-gather | bytes 20480 | tf_op jit(solution)/shard_map/all_gather | solution.py:59
  156.2 3.1 %collective-permute-start.4 = (bf16[1024,128]{1,0:T(8,128)(2,1)S(1)}, bf16[1024,128]{1,0:T(8,128)(2,1)S(1)}, u32[]{:S(2)}, u32[]{:S(2)}) collective-permute-start(bf16[1024,128]{1,0:T(8,128)(2,1)S(1)} %fusion.7), channel_id=1, source_target_pairs={{0,4},{4,8},{8,12},{12,16},{16,20},{20,24},{24,28},{28,32},{32,36}... | collective-permute-start | bytes 786440 | tf_op jit(solution)/shard_map/ppermute | solution.py:15
  159.3 13.0 %collective-permute-start.6 = (bf16[1024,128]{1,0:T(8,128)(2,1)S(1)}, bf16[1024,128]{1,0:T(8,128)(2,1)S(1)}, u32[]{:S(2)}, u32[]{:S(2)}) collective-permute-start(bf16[1024,128]{1,0:T(8,128)(2,1)S(1)} %fusion.7), channel_id=1, source_target_pairs={{0,508},{4,0},{8,4},{12,8},{16,12},{20,16},{24,20},{28,24},{32,28}... | collective-permute-start | bytes 786440 | tf_op jit(solution)/shard_map/ppermute | solution.py:15
  172.3 4.3 %collective-permute-done.4 = bf16[1024,128]{1,0:T(8,128)(2,1)S(1)} collective-permute-done((bf16[1024,128]{1,0:T(8,128)(2,1)S(1)}, bf16[1024,128]{1,0:T(8,128)(2,1)S(1)}, u32[]{:S(2)}, u32[]{:S(2)}) %collective-permute-start.4) | collective-permute-done | bytes 262176 | tf_op jit(solution)/shard_map/ppermute | solution.py:15
  176.6 1.9 collective-permute-start.5
  178.6 14.2 %collective-permute-start.7 = (bf16[1024,128]{1,0:T(8,128)(2,1)S(1)}, bf16[1024,128]{1,0:T(8,128)(2,1)S(1)}, u32[]{:S(2)}, u32[]{:S(2)}) collective-permute-start(bf16[1024,128]{1,0:T(8,128)(2,1)S(1)} %collective-permute-done.6), channel_id=1, source_target_pairs={{0,508},{4,0},{8,4},{12,8},{16,12},{20,16},{24,20},{28,24},{32,28}... | collective-permute-start | bytes 786440 | tf_op jit(solution)/shard_map/ppermute | solution.py:15
  192.8 3.4 %collective-permute-done.5 = bf16[1024,128]{1,0:T(8,128)(2,1)S(1)} collective-permute-done((bf16[1024,128]{1,0:T(8,128)(2,1)S(1)}, bf16[1024,128]{1,0:T(8,128)(2,1)S(1)}, u32[]{:S(2)}, u32[]{:S(2)}) %collective-permute-start.5) | collective-permute-done | bytes 262176 | tf_op jit(solution)/shard_map/ppermute | solution.py:15
  197.6 0.9 constant_dynamic-update-slice_fusion.7
  199.9 3.2 %gather_fusion.1 = bf16[40,128,128]{2,1,0:T(8,128)(2,1)} fusion(bf16[40,128,128]{2,1,0:T(8,128)(2,1)} %bitcast.11, s32[1024]{0:T(1024)S(1)} %pad_clamp_fusion), kind=kCustom, calls=%fused_computation.1 | custom fusion | bytes 2621600 | tf_op jit(solution)/shard_map/gather | solution.py:62
  203.1 3.4 %convolution_bitcast_fusion = bf16[40,128,128]{1,2,0:T(8,128)(2,1)} fusion(bf16[40,128,128]{2,1,0:T(8,128)(2,1)} %gather_fusion.1, s32[1,40,128,128]{3,2,1,0:T(8,128)S(1)} %copy-done), kind=kOutput, calls=%fused_computation.2 | convolution fusion | flops 168427520 | bytes 5242880 | tf_op jit(solution)/shard_map/kij,kjf->kif/dot_general | solution.py:63
  206.5 2.1 copy.25
  209.7 0.8 fusion.8
  210.5 52.1 %all-gather.7.cloned.1.call-done = bf16[1024,512]{1,0:T(8,128)(2,1)} async-done(((bf16[1024,128]{1,0:T(8,128)(2,1)}), bf16[1024,512]{1,0:T(8,128)(2,1)}) %all-gather.7.cloned.1.call-update) | async-done | bytes 1048592 | tf_op jit(solution)/shard_map/all_gather | solution.py:36
  262.6 2.4 convolution_convert_fusion
  (43 shorter events, 6.2 us)
Async XLA Ops:
  7.2 63.0 %copy-start.1 = (bf16[1024,128]{1,0:T(8,128)(2,1)S(1)}, bf16[1024,128]{1,0:T(8,128)(2,1)}, u32[]{:S(2)}) copy-start(bf16[1024,128]{1,0:T(8,128)(2,1)} %param.7) | copy-start | bytes 786436
  7.2 133.1 %all-gather.5.cloned.1.call-start = ((), (), s32[]{:S(2)}) async-start(), calls=%async_computation | async-start | bytes 1310720 | tf_op jit(solution)/shard_map/all_gather | solution.py:36
  30.2 20.4 %collective-permute-start = (bf16[1024,128]{1,0:T(8,128)(2,1)S(1)}, bf16[1024,128]{1,0:T(8,128)(2,1)S(1)}, u32[]{:S(2)}, u32[]{:S(2)}) collective-permute-start(bf16[1024,128]{1,0:T(8,128)(2,1)S(1)} %fusion.5), channel_id=1, source_target_pairs={{0,4},{4,8},{8,12},{12,16},{16,20},{20,24},{24,28},{28,32},{32,36}... | collective-permute-start | bytes 786440 | tf_op jit(solution)/shard_map/ppermute | solution.py:15
  32.1 21.8 %collective-permute-start.2 = (bf16[1024,128]{1,0:T(8,128)(2,1)S(1)}, bf16[1024,128]{1,0:T(8,128)(2,1)S(1)}, u32[]{:S(2)}, u32[]{:S(2)}) collective-permute-start(bf16[1024,128]{1,0:T(8,128)(2,1)S(1)} %fusion.5), channel_id=1, source_target_pairs={{0,508},{4,0},{8,4},{12,8},{16,12},{20,16},{24,20},{28,24},{32,28}... | collective-permute-start | bytes 786440 | tf_op jit(solution)/shard_map/ppermute | solution.py:15
  50.6 19.5 %collective-permute-start.1 = (bf16[1024,128]{1,0:T(8,128)(2,1)S(1)}, bf16[1024,128]{1,0:T(8,128)(2,1)S(1)}, u32[]{:S(2)}, u32[]{:S(2)}) collective-permute-start(bf16[1024,128]{1,0:T(8,128)(2,1)S(1)} %collective-permute-done), channel_id=1, source_target_pairs={{0,4},{4,8},{8,12},{12,16},{16,20},{20,24},{24,28},{28,32},{32,36}... | collective-permute-start | bytes 786440 | tf_op jit(solution)/shard_map/ppermute | solution.py:15
  53.9 18.5 %collective-permute-start.3 = (bf16[1024,128]{1,0:T(8,128)(2,1)S(1)}, bf16[1024,128]{1,0:T(8,128)(2,1)S(1)}, u32[]{:S(2)}, u32[]{:S(2)}) collective-permute-start(bf16[1024,128]{1,0:T(8,128)(2,1)S(1)} %collective-permute-done.2), channel_id=1, source_target_pairs={{0,508},{4,0},{8,4},{12,8},{16,12},{20,16},{24,20},{28,24},{32,28}... | collective-permute-start | bytes 786440 | tf_op jit(solution)/shard_map/ppermute | solution.py:15
  72.4 1.1 copy-start.2
  73.5 3.4 %copy-start = (s32[1,40,128,128]{3,2,1,0:T(8,128)S(1)}, s32[1,40,128,128]{3,2,1,0:T(8,128)}, u32[]{:S(2)}) copy-start(s32[1,40,128,128]{3,2,1,0:T(8,128)} %param.13) | copy-start | bytes 7864324
  80.2 2.8 %copy-start.6 = (s32[1,40]{1,0:T(1,128)S(1)}, s32[1,40]{1,0:T(1,128)}, u32[]{:S(2)}) copy-start(s32[1,40]{1,0:T(1,128)} %param.10) | copy-start | bytes 484
  83.0 1.8 copy-start.4
  85.6 177.0 %all-gather.7.cloned.1.call-start = ((), (), s32[]{:S(2)}) async-start(), calls=%async_computation.1 | async-start | bytes 1310720 | tf_op jit(solution)/shard_map/all_gather | solution.py:36
  142.0 57.2 %copy-start.3 = (bf16[1024,128]{1,0:T(8,128)(2,1)}, bf16[1024,128]{1,0:T(8,128)(2,1)S(1)}, u32[]{:S(2)}) copy-start(bf16[1024,128]{1,0:T(8,128)(2,1)S(1)} %get-tuple-element.5) | copy-start | bytes 786436
  156.2 20.4 %collective-permute-start.4 = (bf16[1024,128]{1,0:T(8,128)(2,1)S(1)}, bf16[1024,128]{1,0:T(8,128)(2,1)S(1)}, u32[]{:S(2)}, u32[]{:S(2)}) collective-permute-start(bf16[1024,128]{1,0:T(8,128)(2,1)S(1)} %fusion.7), channel_id=1, source_target_pairs={{0,4},{4,8},{8,12},{12,16},{16,20},{20,24},{24,28},{28,32},{32,36}... | collective-permute-start | bytes 786440 | tf_op jit(solution)/shard_map/ppermute | solution.py:15
  159.3 19.2 %collective-permute-start.6 = (bf16[1024,128]{1,0:T(8,128)(2,1)S(1)}, bf16[1024,128]{1,0:T(8,128)(2,1)S(1)}, u32[]{:S(2)}, u32[]{:S(2)}) collective-permute-start(bf16[1024,128]{1,0:T(8,128)(2,1)S(1)} %fusion.7), channel_id=1, source_target_pairs={{0,508},{4,0},{8,4},{12,8},{16,12},{20,16},{24,20},{28,24},{32,28}... | collective-permute-start | bytes 786440 | tf_op jit(solution)/shard_map/ppermute | solution.py:15
  176.6 19.5 %collective-permute-start.5 = (bf16[1024,128]{1,0:T(8,128)(2,1)S(1)}, bf16[1024,128]{1,0:T(8,128)(2,1)S(1)}, u32[]{:S(2)}, u32[]{:S(2)}) collective-permute-start(bf16[1024,128]{1,0:T(8,128)(2,1)S(1)} %collective-permute-done.4), channel_id=1, source_target_pairs={{0,4},{4,8},{8,12},{12,16},{16,20},{20,24},{24,28},{28,32},{32,36}... | collective-permute-start | bytes 786440 | tf_op jit(solution)/shard_map/ppermute | solution.py:15
  178.6 20.6 %collective-permute-start.7 = (bf16[1024,128]{1,0:T(8,128)(2,1)S(1)}, bf16[1024,128]{1,0:T(8,128)(2,1)S(1)}, u32[]{:S(2)}, u32[]{:S(2)}) collective-permute-start(bf16[1024,128]{1,0:T(8,128)(2,1)S(1)} %collective-permute-done.6), channel_id=1, source_target_pairs={{0,508},{4,0},{8,4},{12,8},{16,12},{20,16},{24,20},{28,24},{32,28}... | collective-permute-start | bytes 786440 | tf_op jit(solution)/shard_map/ppermute | solution.py:15
  208.7 1.0 copy-start.5
Sparse Core Ops, SparseCore 0:
  85.7 54.4 all-gather.4
  210.6 51.9 all-gather.6
